TPU v7x, 32 devices: a whole 2x2x4 slice. The times are simulated.
32 devices in a mesh: row: 8 (over z, x), col: 4 (over y, core).
Axes of the slice: x: 2, y: 2, z: 4, core: 2. Of those that a mesh axis runs over, the one named last changes fastest.
Arguments:
- hidden: bfloat16 [8192, 1600], P('row', 'col'), may hold values from -60 to 60
- up_weight: bfloat16 [1600, 6400], P('row', 'col'), may hold values from -0.15625 to 0.15625
- up_bias: float32 [6400], P('col'), may hold values from -3 to 3
- down_weight: bfloat16 [6400, 1600], P('col', 'row'), may hold values from -0.078125 to 0.078125
- down_bias: float32 [1600], P('col'), may hold values from -3 to 3
- query_key_value_weight: bfloat16 [1600, 4800], P('row', 'col'), may hold values from -0.15625 to 0.15625
- query_key_value_bias: float32 [4800], P('col'), may hold values from -3 to 3
- block_norm_gain: float32 [1600], replicated, may hold values from 0.1 to 1.9
- block_norm_shift: float32 [1600], replicated, may hold values from -3 to 3
- following_norm_gain: float32 [1600], replicated, may hold values from 0.1 to 1.9
- following_norm_shift: float32 [1600], replicated, may hold values from -3 to 3
- up_down_factors: bfloat16 [32, 16, 1600], P('row'), may hold values from -0.15625 to 0.15625
- up_up_factors: bfloat16 [32, 16, 6400], P('row', None, 'col'), may hold values from -1.5 to 1.5
- query_key_value_down_factors: bfloat16 [32, 16, 1600], P('row'), may hold values from -0.15625 to 0.15625
- query_key_value_up_factors: bfloat16 [32, 16, 4800], P('row', None, 'col'), may hold values from -1.5 to 1.5
- adapter_storage_slot: int32 [32], replicated, may hold values from 0 to 31, as said below
- tile_adapter_index: int32 [64], P('row'), may hold values from 0 to 31, as said below
- tile_token_rows: int32 [64], P('row'), may hold values from 1 to 128, as said below
Outputs:
- h_out: bfloat16 [8192, 1600], P('row', 'col')
- qkv: bfloat16 [8192, 4800], P('row', 'col')
Inputs may be any that keep to these rules, and one draw needn't show every extreme that they name: A permutation: adapter a is stored in slot adapter_storage_slot[a], and index r of row holds slots r * 4 to (r + 1) * 4 - 1. `tile_adapter_index`: the 8 tiles of one index of row name adapters whose slots lie on distinct indices of row. A tile's first tile_token_rows rows are prompt tokens, the rest padding.
All inputs are finite; a program needn't handle non-finite values.
Results may differ from a plain program's by a relative error of at most 0.02.
Values may be sent and summed in bfloat16 or wider, within the bound.
A program may use at most 64 MiB of HBM per device.

v0:
```python
import jax
import jax.numpy as jnp
from jax import lax
from jax.sharding import PartitionSpec as P


def layer_norm(values, gain_vec, shift_vec):
    row_mean = jnp.mean(values, axis=-1, keepdims=True)
    centred = values - row_mean
    variance = jnp.mean(centred * centred, axis=-1, keepdims=True)
    return centred * lax.rsqrt(variance + 1e-05) * gain_vec + shift_vec


def fold_rows(operand, weight_piece):
    return jnp.dot(operand, weight_piece, preferred_element_type=jnp.float32)


def adapter_update(
    normalized_input, down_factor, up_factor, holder_row, resident_slot, tile_total_count
):
    tok_rows, feat_width = normalized_input.shape
    tile_len = tok_rows // tile_total_count
    per_holder, adapter_rank_size, unused_result = down_factor.shape
    tiled_rows = normalized_input.reshape(tile_total_count, tile_len, feat_width)
    owners = lax.axis_size("row")
    select = (holder_row[None, :] == jnp.arange(owners, dtype=jnp.int32)[:, None]).astype(
        jnp.bfloat16
    )
    slot_pick = (resident_slot[:, None] == jnp.arange(per_holder, dtype=jnp.int32)[None, :]).astype(
        jnp.bfloat16
    )
    outgoing = jnp.einsum(
        "ot,tid->oid", select, tiled_rows, preferred_element_type=jnp.float32
    ).astype(jnp.bfloat16)
    labels = jnp.dot(select, slot_pick, preferred_element_type=jnp.float32).astype(jnp.bfloat16)
    received_rows, slot_marks = (
        lax.all_to_all(outgoing, "row", split_axis=0, concat_axis=0, tiled=True),
        lax.all_to_all(labels, "row", split_axis=0, concat_axis=0, tiled=True),
    )
    every_low_rank = jnp.einsum(
        "kph,fch->kpfc", received_rows, down_factor, preferred_element_type=jnp.float32
    )
    low_rank = jnp.sum(
        every_low_rank * slot_marks.astype(jnp.float32)[:, None, :, None], axis=2
    ).astype(jnp.bfloat16)
    broadcast_rows = (low_rank[:, :, None, :] * slot_marks[:, None, :, None]).reshape(
        owners, tile_len, per_holder * adapter_rank_size
    )
    answer = jnp.einsum(
        "sik,kf->sif",
        broadcast_rows,
        up_factor.reshape(per_holder * adapter_rank_size, -1),
        preferred_element_type=jnp.float32,
    ).astype(jnp.bfloat16)
    returned = lax.all_to_all(answer, "row", split_axis=0, concat_axis=0, tiled=True)
    update_rows = jnp.einsum(
        "ot,oif->tif", select, returned, preferred_element_type=jnp.float32
    ).astype(jnp.bfloat16)
    update_rows = lax.optimization_barrier(update_rows)
    return update_rows.reshape(tok_rows, -1).astype(jnp.float32)


def per_device(
    hidden,
    up_weight,
    up_bias,
    down_weight,
    down_bias,
    query_key_value_weight,
    query_key_value_bias,
    block_norm_gain,
    block_norm_shift,
    following_norm_gain,
    following_norm_shift,
    up_down_factors,
    up_up_factors,
    query_key_value_down_factors,
    query_key_value_up_factors,
    adapter_storage_slot,
    tile_adapter_index,
    tile_token_rows,
):
    tok_rows = hidden.shape[0]
    tile_total_count = tile_adapter_index.shape[0]
    tile_len = tok_rows // tile_total_count
    per_holder = up_down_factors.shape[0]
    adapter_count = adapter_storage_slot.shape[0]
    adapter_pick = (
        tile_adapter_index[:, None] == jnp.arange(adapter_count, dtype=jnp.int32)[None, :]
    ).astype(jnp.int32)
    slot_ids = jnp.sum(adapter_pick * adapter_storage_slot[None, :], axis=1)
    holder_row = slot_ids // per_holder
    resident_slot = slot_ids % per_holder
    valid = (jnp.arange(tile_len, dtype=jnp.int32)[None, :] < tile_token_rows[:, None]).reshape(
        tok_rows, 1
    )
    gathered = lax.all_gather(hidden, "col", axis=1, tiled=True)
    normalized_input = layer_norm(
        gathered.astype(jnp.float32), block_norm_gain, block_norm_shift
    ).astype(jnp.bfloat16)
    up_dense = fold_rows(normalized_input, lax.all_gather(up_weight, "row", axis=0, tiled=True))
    up_projection = (
        up_dense
        + up_bias
        + adapter_update(
            normalized_input,
            up_down_factors,
            up_up_factors,
            holder_row,
            resident_slot,
            tile_total_count,
        )
    )
    activated = jax.nn.gelu(up_projection, approximate=True).astype(jnp.bfloat16)
    partial_value = jnp.dot(
        activated,
        lax.all_gather(down_weight, "row", axis=1, tiled=True),
        preferred_element_type=jnp.float32,
    )
    summed = lax.psum_scatter(
        partial_value.astype(jnp.bfloat16), "col", scatter_dimension=1, tiled=True
    ).astype(jnp.float32)
    mixed = hidden.astype(jnp.float32) + summed + down_bias
    h_out = jnp.where(valid, mixed, 0.0).astype(jnp.bfloat16)
    gathered_next = lax.all_gather(h_out, "col", axis=1, tiled=True)
    normalized_following = layer_norm(
        gathered_next.astype(jnp.float32), following_norm_gain, following_norm_shift
    ).astype(jnp.bfloat16)
    qkv_dense = fold_rows(
        normalized_following, lax.all_gather(query_key_value_weight, "row", axis=0, tiled=True)
    )
    projected_output = (
        qkv_dense
        + query_key_value_bias
        + adapter_update(
            normalized_following,
            query_key_value_down_factors,
            query_key_value_up_factors,
            holder_row,
            resident_slot,
            tile_total_count,
        )
    )
    qkv = jnp.where(valid, projected_output, 0.0).astype(jnp.bfloat16)
    return (h_out, qkv)


def solution(mesh):
    in_specs = (
        P("row", "col"),
        P("row", "col"),
        P("col"),
        P("col", "row"),
        P("col"),
        P("row", "col"),
        P("col"),
        P(),
        P(),
        P(),
        P(),
        P("row", None, None),
        P("row", None, "col"),
        P("row", None, None),
        P("row", None, "col"),
        P(),
        P("row"),
        P("row"),
    )
    out_specs = (P("row", "col"), P("row", "col"))
    return jax.shard_map(
        per_device, mesh=mesh, in_specs=in_specs, out_specs=out_specs, check_vma=False
    )
```

profile of v0, /device:TPU:0, one launch (start us, length us, event | category | flops | bytes accessed | tf_op | source)
XLA Modules:
  0.0 654.0 jit_solution(14058357577489934825)
XLA Ops:
  7.2 0.0 copy-start
  7.2 0.0 copy-start.7
  7.2 0.0 copy-start.6
  7.2 0.0 all-gather.6.cloned.1.call-start
  7.2 0.7 all-gather.6.cloned.1.call-update
  7.9 0.0 all-gather.8.cloned.1.call-start
  8.0 0.7 all-gather.8.cloned.1.call-update
  8.7 0.9 select_reduce_fusion
  9.6 0.3 fusion.48
  9.8 0.7 copy.30
  10.5 7.3 %all-to-all-start.1 = ((bf16[8,1,4]{2,1,0:T(2,128)(2,1)}), bf16[8,1,4]{2,1,0:T(2,128)(2,1)S(1)}, u32[]{:S(2)}, u32[]{:S(2)}) async-start(bf16[8,1,4]{2,1,0:T(2,128)(2,1)} %copy.30), calls=%async_computation.1 | async-start | bytes 8192 | tf_op jit(solution)/shard_map/all_to_all | solution.py:38
  17.8 23.9 %all-gather.6.cloned.1.call-done = bf16[1024,1600]{0,1:T(8,128)(2,1)} async-done(((bf16[1024,400]{0,1:T(8,128)(2,1)}), bf16[1024,1600]{0,1:T(8,128)(2,1)}) %all-gather.6.cloned.1.call-update) | async-done | bytes 3276816 | tf_op jit(solution)/shard_map/all_gather | solution.py:97
  41.6 2.7 convert_reduce_fusion.1
  44.3 0.2 copy-done.2
  44.5 0.9 fusion.8
  45.4 0.0 copy-done.7
  45.4 0.0 copy-done.6
  45.5 1.6 fusion.75
  47.1 0.9 copy.46
  48.0 1.4 convolution_convert_fusion.2
  49.4 2.3 copy.29
  51.7 0.0 all-to-all-done.1
  51.7 5.5 all-to-all-start
  57.2 0.0 all-gather.10.cloned.1.call-start
  57.2 0.7 all-gather.10.cloned.1.call-update
  57.9 0.0 reduce-scatter.2.cloned.1.call-start
  58.0 0.1 copy.31
  58.1 0.1 copy.32
  58.1 0.1 copy.33
  58.2 127.9 %all-to-all-done = bf16[8,128,1600]{1,2,0:T(8,128)(2,1)} async-done(((bf16[8,128,1600]{1,2,0:T(8,128)(2,1)}), bf16[8,128,1600]{1,2,0:T(8,128)(2,1)}, u32[]{:S(2)}, u32[]{:S(2)}) %all-to-all-start) | async-done | bytes 3276832 | tf_op jit(solution)/shard_map/all_to_all | solution.py:37
  186.1 2.6 fusion.45
  188.8 1.1 bitcast_convert_fusion
  189.9 138.7 %all_to_all.33 = bf16[8,128,1600]{1,2,0:T(8,128)(2,1)S(1)} all-to-all(bf16[8,128,1600]{1,2,0:T(8,128)(2,1)S(1)} %bitcast_convert_fusion), channel_id=1, replica_groups=mesh['row'=8,'col'=4] {'row'}, dimensions={0} | all-to-all | bytes 6553600 | tf_op jit(solution)/shard_map/all_to_all | solution.py:55
  328.5 2.0 fusion.30
  330.6 0.0 copy-start.11
  330.6 2.9 convert_element_type.115
  333.5 14.9 %fusion.19.clone.4 = bf16[1024,1600]{0,1:T(8,128)(2,1)} fusion(f32[200,8,8,128]{3,2,1,0:T(8,128)} %bitcast.93, bf16[1600,1600]{1,0:T(8,128)(2,1)} %all-gather.8.cloned.1.call-done, f32[1600]{0:T(1024)S(1)} %copy-done.11, bf16[1024,1600]{0,1:T(8,128)(2,1)S(1)} %copy-done.2, f32[1600]{0:T(1024)S(1)} %copy-done.6, f32[1600]{0:T(1024)S(1)} %copy-done.7, ...), kind=kOutput, calls=%fused_computation.24.clone.clone.clone.1 | convolution fusion | flops 5270732800 | bytes 18254592 | tf_op jit(solution)/shard_map/dot_general | solution.py:15
  348.4 0.0 all-gather.10.cloned.1.call-done
  348.4 10.8 %convolution_convert_fusion = bf16[1024,1600]{0,1:T(8,128)(2,1)} fusion(bf16[1600,1600]{0,1:T(8,128)(2,1)} %all-gather.10.cloned.1.call-done, bf16[1024,1600]{0,1:T(8,128)(2,1)} %fusion.19.clone.4), kind=kOutput, calls=%fused_computation.31 | convolution fusion | flops 5244518400 | bytes 11673600 | tf_op jit(solution)/shard_map/dot_general | solution.py:115
  359.3 0.0 reduce-scatter.2.cloned.1.call-update
  359.3 0.0 all-gather.12.cloned.1.call-start
  359.3 0.1 fusion.64
  359.4 38.2 %reduce-scatter.2.cloned.1.call-done = bf16[1024,400]{0,1:T(8,128)(2,1)} async-done(((bf16[1024,1600]{0,1:T(8,128)(2,1)}), bf16[1024,400]{0,1:T(8,128)(2,1)}) %reduce-scatter.2.cloned.1.call-update) | async-done | bytes 819216 | tf_op jit(solution)/shard_map/reduce_scatter | solution.py:120
  397.7 2.3 select_convert_fusion
  400.0 0.0 all-gather.12.cloned.1.call-update
  400.0 29.4 %all-gather.12.cloned.1.call-done = bf16[1024,1600]{0,1:T(8,128)(2,1)} async-done(((bf16[1024,400]{0,1:T(8,128)(2,1)}), bf16[1024,1600]{0,1:T(8,128)(2,1)}) %all-gather.12.cloned.1.call-update) | async-done | bytes 3276816 | tf_op jit(solution)/shard_map/all_gather | solution.py:125
  429.5 2.7 convert_reduce_fusion
  432.2 0.2 copy-done.3
  432.4 0.9 fusion.4
  433.3 1.6 fusion.78
  435.0 0.9 copy.48
  435.8 1.4 convolution_convert_fusion.1
  437.3 2.2 copy.36
  439.5 5.6 all-to-all-start.3
  445.1 0.0 all-gather.14.cloned.1.call-start
  445.2 0.5 all-gather.14.cloned.1.call-update
  445.7 123.2 %all-to-all-done.3 = bf16[8,128,1600]{1,2,0:T(8,128)(2,1)} async-done(((bf16[8,128,1600]{1,2,0:T(8,128)(2,1)}), bf16[8,128,1600]{1,2,0:T(8,128)(2,1)}, u32[]{:S(2)}, u32[]{:S(2)}) %all-to-all-start.3) | async-done | bytes 3276832 | tf_op jit(solution)/shard_map/all_to_all | solution.py:37
  568.9 2.6 fusion.42
  571.6 1.8 bitcast_convert_fusion.1
  573.4 59.6 %all_to_all.34 = bf16[8,128,1200]{1,2,0:T(8,128)(2,1)S(1)} all-to-all(bf16[8,128,1200]{1,2,0:T(8,128)(2,1)S(1)} %bitcast_convert_fusion.1), channel_id=1, replica_groups=mesh['row'=8,'col'=4] {'row'}, dimensions={0} | all-to-all | bytes 4915200 | tf_op jit(solution)/shard_map/all_to_all | solution.py:55
  633.0 0.8 fusion.33
  633.9 0.0 copy-start.12
  633.9 2.4 convert_element_type.116
  636.3 10.9 %fusion.21 = bf16[1024,1200]{0,1:T(8,128)(2,1)} fusion(f32[150,8,8,128]{3,2,1,0:T(8,128)} %bitcast.94, bf16[1600,1200]{1,0:T(8,128)(2,1)} %all-gather.14.cloned.1.call-done, f32[1200]{0:T(1024)S(1)} %copy-done.12, pred[1024]{0:T(1024)(128)(4,1)S(1)} %fusion.64, bf16[1024,1600]{0,1:T(8,128)(2,1)S(1)} %copy-done.3, f32[1600]{0:T(1024)S(1)} %copy-done.8, ...), kind=kOutput, calls=%fused_computation.29 | convolution fusion | flops 3946905600 | bytes 14516416 | tf_op jit(solution)/shard_map/dot_general | solution.py:15
  (27 shorter events, 0.1 us)
Async XLA Ops:
  7.2 181.6 %copy-start = (bf16[4,16,1600]{2,1,0:T(8,128)(2,1)S(1)}, bf16[4,16,1600]{2,1,0:T(8,128)(2,1)}, u32[]{:S(2)}) copy-start(bf16[4,16,1600]{2,1,0:T(8,128)(2,1)} %param.30) | copy-start | bytes 614404
  7.2 38.3 %copy-start.7 = (f32[1600]{0:T(1024)S(1)}, f32[1600]{0:T(1024)}, u32[]{:S(2)}) copy-start(f32[1600]{0:T(1024)} %param.25) | copy-start | bytes 19204
  7.2 38.3 %copy-start.6 = (f32[1600]{0:T(1024)S(1)}, f32[1600]{0:T(1024)}, u32[]{:S(2)}) copy-start(f32[1600]{0:T(1024)} %param.26) | copy-start | bytes 19204
  7.2 34.4 %all-gather.6.cloned.1.call-start = ((), (), s32[]{:S(2)}) async-start(), calls=%async_computation.6 | async-start | bytes 4096000 | tf_op jit(solution)/shard_map/all_gather | solution.py:97
  7.9 325.6 %all-gather.8.cloned.1.call-start = ((), (), s32[]{:S(2)}) async-start(), calls=%async_computation.7 | async-start | bytes 5990400 | tf_op jit(solution)/shard_map/all_gather | solution.py:101
  10.5 41.2 %all-to-all-start.1 = ((bf16[8,1,4]{2,1,0:T(2,128)(2,1)}), bf16[8,1,4]{2,1,0:T(2,128)(2,1)S(1)}, u32[]{:S(2)}, u32[]{:S(2)}) async-start(bf16[8,1,4]{2,1,0:T(2,128)(2,1)} %copy.30), calls=%async_computation.1 | async-start | bytes 8192 | tf_op jit(solution)/shard_map/all_to_all | solution.py:38
  41.6 2.9 copy-start.2
  51.7 134.4 %all-to-all-start = ((bf16[8,128,1600]{1,2,0:T(8,128)(2,1)}), bf16[8,128,1600]{1,2,0:T(8,128)(2,1)}, u32[]{:S(2)}, u32[]{:S(2)}) async-start(bf16[8,128,1600]{1,2,0:T(8,128)(2,1)} %copy.29), calls=%async_computation | async-start | bytes 6553600 | tf_op jit(solution)/shard_map/all_to_all | solution.py:37
  57.2 291.3 %all-gather.10.cloned.1.call-start = ((), (), s32[]{:S(2)}) async-start(), calls=%async_computation.8 | async-start | bytes 5990400 | tf_op jit(solution)/shard_map/all_gather | solution.py:117
  57.9 339.8 %reduce-scatter.2.cloned.1.call-start = ((), (), s32[]{:S(2)}) async-start(), calls=%async_computation.9 | async-start | bytes 4096000 | tf_op jit(solution)/shard_map/reduce_scatter | solution.py:120
  330.6 3.0 copy-start.11
  348.4 10.9 %copy-start.13 = (s32[8]{0:T(128)S(1)}, s32[8]{0:T(128)}, u32[]{:S(2)}) copy-start(s32[8]{0:T(128)} %param.35) | copy-start | bytes 100
  348.4 49.2 %copy-start.4 = (bf16[1024,400]{0,1:T(8,128)(2,1)S(1)}, bf16[1024,400]{0,1:T(8,128)(2,1)}, u32[]{:S(2)}) copy-start(bf16[1024,400]{0,1:T(8,128)(2,1)} %param.18) | copy-start | bytes 2457604
  348.4 49.3 %copy-start.10 = (f32[400]{0:T(512)S(1)}, f32[400]{0:T(512)}, u32[]{:S(2)}) copy-start(f32[400]{0:T(512)} %param.22) | copy-start | bytes 4804
  359.3 70.2 %all-gather.12.cloned.1.call-start = ((), (), s32[]{:S(2)}) async-start(), calls=%async_computation.10 | async-start | bytes 4096000 | tf_op jit(solution)/shard_map/all_gather | solution.py:125
  359.4 73.9 %copy-start.8 = (f32[1600]{0:T(1024)S(1)}, f32[1600]{0:T(1024)}, u32[]{:S(2)}) copy-start(f32[1600]{0:T(1024)} %param.28) | copy-start | bytes 19204
  359.4 73.9 %copy-start.9 = (f32[1600]{0:T(1024)S(1)}, f32[1600]{0:T(1024)}, u32[]{:S(2)}) copy-start(f32[1600]{0:T(1024)} %param.27) | copy-start | bytes 19204
  429.5 2.9 copy-start.3
  439.5 129.5 %copy-start.5 = (bf16[4,16,1600]{2,1,0:T(8,128)(2,1)S(1)}, bf16[4,16,1600]{2,1,0:T(8,128)(2,1)}, u32[]{:S(2)}) copy-start(bf16[4,16,1600]{2,1,0:T(8,128)(2,1)} %param.31) | copy-start | bytes 614404
  439.5 129.5 %all-to-all-start.3 = ((bf16[8,128,1600]{1,2,0:T(8,128)(2,1)}), bf16[8,128,1600]{1,2,0:T(8,128)(2,1)}, u32[]{:S(2)}, u32[]{:S(2)}) async-start(bf16[8,128,1600]{1,2,0:T(8,128)(2,1)} %copy.36), calls=%async_computation.4 | async-start | bytes 6553600 | tf_op jit(solution)/shard_map/all_to_all | solution.py:37
  445.1 191.2 %all-gather.14.cloned.1.call-start = ((), (), s32[]{:S(2)}) async-start(), calls=%async_computation.11 | async-start | bytes 4608000 | tf_op jit(solution)/shard_map/all_gather | solution.py:130
  633.9 2.4 copy-start.12
  636.3 10.9 %copy-start.1 = (bf16[4,16,1600]{2,1,0:T(8,128)(2,1)S(1)}, bf16[4,16,1600]{2,1,0:T(8,128)(2,1)}, u32[]{:S(2)}) copy-start(bf16[4,16,1600]{2,1,0:T(8,128)(2,1)} %param.30) | copy-start | bytes 614404
Sparse Core Ops, SparseCore 0:
  9.6 31.9 all-gather.5
  43.8 147.3 all-gather.7
  193.4 137.5 all-gather.9
  359.4 38.2 reduce-scatter.1
  400.2 29.2 all-gather.11
  448.1 123.5 all-gather.13
where the time goes:
time: 655 us; the launch traced here: 654 us
  waiting for transfers between devices  345 us (53%)
  blocking collectives  198 us (30%)
  matrix products  50.8 us (8%)
  other arithmetic  19.1 us (3%)
  starting transfers between devices  18.6 us (3%)
  between operations  14.3 us (2%)
  local copies, waits for them, and re-layouts  7.61 us (1%)
    all_to_all x2, waiting for transfers between devices, adapter_update(): lax.all_to_all(outgoing, 'row', split_axis=0, concat_axis=0, tiled=True)  251 us
    all_to_all x2, blocking collectives, adapter_update(): lax.all_to_all(answer, 'row', split_axis=0, concat_axis=0, tiled=True)  198 us
    reduce_scatter x1, waiting for transfers between devices, per_device(): lax.psum_scatter(partial_value.astype(jnp.bfloat16), 'col', scatter_dimen...  38.2 us
    all_gather x1, waiting for transfers between devices, per_device(): gathered_next = lax.all_gather(h_out, 'col', axis=1, tiled=True)  29.4 us
    dot_general x2, matrix products, fold_rows(): return jnp.dot(operand, weight_piece, preferred_element_type=jnp.float32)  25.8 us
    all_gather x1, waiting for transfers between devices, per_device(): gathered = lax.all_gather(hidden, 'col', axis=1, tiled=True)  23.9 us
  transfers between devices with their start and end apart: 9, of which 5 were waited for; matrix products, arithmetic and copies ran while one was open for 7% of the time, Pallas kernels for 0%

commit v1 on v0

--- a/solution.py
+++ b/solution.py
@@ -2,6 +2,7 @@
 import jax.numpy as jnp
 from jax import lax
 from jax.sharding import PartitionSpec as P
+from jax.lax import axis_index, ppermute, psum
 
 
 def layer_norm(values, gain_vec, shift_vec):
@@ -80,6 +81,24 @@
     tile_adapter_index,
     tile_token_rows,
 ):
+
+    def pair_tables(page, shard_axis, axis_k):
+        world_n = psum(1, shard_axis)
+        after = range(world_n)
+        upper = map(lambda pp: (pp, (pp + 1) % world_n), after)
+        inbox = list(upper)
+
+        def racks_switch(tile_out):
+            if len(tile_out) == world_n:
+                return tile_out
+            r_now = ppermute(tile_out[0], shard_axis, perm=inbox)
+            return racks_switch([r_now, *tile_out])
+
+        fresh = racks_switch([page])
+        y = jnp.concatenate(fresh, axis=axis_k)
+        earlier = axis_index(shard_axis)
+        return jnp.roll(y, (earlier + 1) * page.shape[axis_k], axis_k)
+
     tok_rows = hidden.shape[0]
     tile_total_count = tile_adapter_index.shape[0]
     tile_len = tok_rows // tile_total_count
@@ -94,7 +113,7 @@
     valid = (jnp.arange(tile_len, dtype=jnp.int32)[None, :] < tile_token_rows[:, None]).reshape(
         tok_rows, 1
     )
-    gathered = lax.all_gather(hidden, "col", axis=1, tiled=True)
+    gathered = pair_tables(hidden, "col", 1)
     normalized_input = layer_norm(
         gathered.astype(jnp.float32), block_norm_gain, block_norm_shift
     ).astype(jnp.bfloat16)

time: 655 us -> 646 us (0.986)
  waiting for transfers between devices: 345 us -> 335 us
  blocking collectives: 198 us -> 190 us
    ppermute x0 -> x3, waiting for transfers between devices: none -> 27.3 us  [racks_switch(): r_now = ppermute(tile_out[0], shard_axis, perm=inbox)]
    all_gather x1 -> x0, waiting for transfers between devices: 23.9 us -> none  [per_device(): gathered = lax.all_gather(hidden, 'col', axis=1, tiled=True)]
    all_to_all x2, waiting for transfers between devices: 251 us -> 240 us  [adapter_update(): lax.all_to_all(outgoing, 'row', split_axis=0, concat_axis=0, tiled=True)]
    all_to_all x2, blocking collectives: 198 us -> 190 us  [adapter_update(): lax.all_to_all(answer, 'row', split_axis=0, concat_axis=0, tiled=True)]
  transfers between devices with their start and end apart: 9 -> 11, of which waited for: 5 -> 7; matrix products, arithmetic and copies ran while one was open for 7% -> 7% of each run, Pallas kernels for 0% -> 0%
where the time goes in v1:
time: 646 us; the launch traced here: 639 us
  waiting for transfers between devices  335 us (52%)
  blocking collectives  190 us (29%)
  matrix products  51.2 us (8%)
  other arithmetic  20.2 us (3%)
  starting transfers between devices  19.4 us (3%)
  between operations  14.3 us (2%)
  local copies, waits for them, and re-layouts  9.18 us (1%)
    all_to_all x2, waiting for transfers between devices, adapter_update(): lax.all_to_all(outgoing, 'row', split_axis=0, concat_axis=0, tiled=True)  240 us
    all_to_all x2, blocking collectives, adapter_update(): lax.all_to_all(answer, 'row', split_axis=0, concat_axis=0, tiled=True)  190 us
    reduce_scatter x1, waiting for transfers between devices, per_device(): lax.psum_scatter(partial_value.astype(jnp.bfloat16), 'col', scatter_dimen...  37 us
    all_gather x1, waiting for transfers between devices, per_device(): gathered_next = lax.all_gather(h_out, 'col', axis=1, tiled=True)  29.4 us
    dot_general x2, matrix products, fold_rows(): return jnp.dot(operand, weight_piece, preferred_element_type=jnp.float32)  27.3 us
    ppermute x3, waiting for transfers between devices, racks_switch(): r_now = ppermute(tile_out[0], shard_axis, perm=inbox)  27.3 us
  transfers between devices with their start and end apart: 11, of which 7 were waited for; matrix products, arithmetic and copies ran while one was open for 7% of the time, Pallas kernels for 0%

profile of v1, /device:TPU:0, one launch (start us, length us, event | category | flops | bytes accessed | tf_op | source)
XLA Modules:
  0.0 638.7 jit_solution(15890471128266679269)
XLA Ops:
  7.2 0.0 all-gather.5.cloned.1.call-start
  7.2 0.5 collective-permute-start
  7.7 12.2 %collective-permute-done = bf16[1024,400]{0,1:T(8,128)(2,1)S(1)} collective-permute-done((bf16[1024,400]{0,1:T(8,128)(2,1)}, bf16[1024,400]{0,1:T(8,128)(2,1)S(1)}, u32[]{:S(2)}, u32[]{:S(2)}) %collective-permute-start) | collective-permute-done | bytes 819232 | tf_op jit(solution)/shard_map/ppermute | solution.py:94
  19.9 0.0 collective-permute-start.1
  20.0 0.0 all-gather.5.cloned.1.call-update
  20.0 11.7 %collective-permute-done.1 = bf16[1024,400]{0,1:T(8,128)(2,1)S(1)} collective-permute-done((bf16[1024,400]{0,1:T(8,128)(2,1)S(1)}, bf16[1024,400]{0,1:T(8,128)(2,1)S(1)}, u32[]{:S(2)}, u32[]{:S(2)}) %collective-permute-start.1) | collective-permute-done | bytes 819232 | tf_op jit(solution)/shard_map/ppermute | solution.py:94
  31.7 0.9 select_reduce_fusion
  32.6 0.3 fusion.48
  32.8 0.7 copy.30
  33.5 6.6 %all-to-all-start.1 = ((bf16[8,1,4]{2,1,0:T(2,128)(2,1)}), bf16[8,1,4]{2,1,0:T(2,128)(2,1)S(1)}, u32[]{:S(2)}, u32[]{:S(2)}) async-start(bf16[8,1,4]{2,1,0:T(2,128)(2,1)} %copy.30), calls=%async_computation.1 | async-start | bytes 8192 | tf_op jit(solution)/shard_map/all_to_all | solution.py:39
  40.1 3.4 collective-permute-done.2
  43.5 0.1 constant_dynamic-update-slice_fusion.7
  43.5 0.1 constant_dynamic-update-slice_fusion.6
  43.6 0.1 constant_dynamic-update-slice_fusion.5
  43.7 1.2 constant_dynamic-update-slice_fusion.4
  44.9 0.1 constant_dynamic-update-slice_fusion.3
  44.9 0.1 constant_dynamic-update-slice_fusion.2
  45.0 0.1 constant_dynamic-update-slice_fusion.1
  45.1 0.1 constant_dynamic-update-slice_fusion
  45.2 1.0 convert_reduce_fusion.1
  46.1 1.3 fusion.8
  47.5 0.4 copy-done.3
  47.9 2.1 fusion.77
  49.9 0.9 copy.46
  50.8 1.4 convolution_convert_fusion.2
  52.2 2.3 copy.29
  54.5 6.6 %all-to-all-start = ((bf16[8,128,1600]{1,2,0:T(8,128)(2,1)}), bf16[8,128,1600]{1,2,0:T(8,128)(2,1)S(1)}, u32[]{:S(2)}, u32[]{:S(2)}) async-start(bf16[8,128,1600]{1,2,0:T(8,128)(2,1)} %copy.29), calls=%async_computation | async-start | bytes 6553600 | tf_op jit(solution)/shard_map/all_to_all | solution.py:38
  61.1 0.0 all-gather.7.cloned.1.call-start
  61.1 0.7 all-gather.7.cloned.1.call-update
  61.8 0.0 reduce-scatter.2.cloned.1.call-start
  61.9 0.1 copy.31
  62.0 0.1 copy.32
  62.1 0.1 copy.33
  62.2 116.4 %all-to-all-done = bf16[8,128,1600]{1,2,0:T(8,128)(2,1)S(1)} async-done(((bf16[8,128,1600]{1,2,0:T(8,128)(2,1)}), bf16[8,128,1600]{1,2,0:T(8,128)(2,1)S(1)}, u32[]{:S(2)}, u32[]{:S(2)}) %all-to-all-start) | async-done | bytes 3276832 | tf_op jit(solution)/shard_map/all_to_all | solution.py:38
  178.6 1.6 fusion.45
  180.3 1.1 bitcast_convert_fusion
  181.4 129.8 %all_to_all.33 = bf16[8,128,1600]{1,2,0:T(8,128)(2,1)S(1)} all-to-all(bf16[8,128,1600]{1,2,0:T(8,128)(2,1)S(1)} %bitcast_convert_fusion), channel_id=1, replica_groups=mesh['row'=8,'col'=4] {'row'}, dimensions={0} | all-to-all | bytes 6553600 | tf_op jit(solution)/shard_map/all_to_all | solution.py:56
  311.2 2.0 fusion.30
  313.2 3.0 convert_element_type.115
  316.2 16.4 %fusion.19.clone.4 = bf16[1024,1600]{0,1:T(8,128)(2,1)} fusion(f32[200,8,8,128]{3,2,1,0:T(8,128)} %bitcast.93, bf16[1600,1600]{1,0:T(8,128)(2,1)} %all-gather.5.cloned.1.call-done, f32[1600]{0:T(1024)S(1)} %copy-done.12, f32[1600]{0:T(1024)S(1)} %copy-done.7, f32[1600]{0:T(1024)S(1)} %copy-done.8, f32[1024]{0:T(1024)S(1)} %add_rsqrt_fusion.1, ...), kind=kOutput, calls=%fused_computation.24.clone.clone.clone.1 | convolution fusion | flops 5270732800 | bytes 18459396 | tf_op jit(solution)/shard_map/dot_general | solution.py:16
  332.7 10.8 %convolution_convert_fusion = bf16[1024,1600]{0,1:T(8,128)(2,1)} fusion(bf16[1600,1600]{0,1:T(8,128)(2,1)} %all-gather.7.cloned.1.call-done, bf16[1024,1600]{0,1:T(8,128)(2,1)} %fusion.19.clone.4), kind=kOutput, calls=%fused_computation.31 | convolution fusion | flops 5244518400 | bytes 11673600 | tf_op jit(solution)/shard_map/dot_general | solution.py:134
  343.4 0.0 reduce-scatter.2.cloned.1.call-update
  343.4 0.0 all-gather.9.cloned.1.call-start
  343.5 0.1 fusion.64
  343.6 37.0 %reduce-scatter.2.cloned.1.call-done = bf16[1024,400]{0,1:T(8,128)(2,1)} async-done(((bf16[1024,1600]{0,1:T(8,128)(2,1)}), bf16[1024,400]{0,1:T(8,128)(2,1)}) %reduce-scatter.2.cloned.1.call-update) | async-done | bytes 819216 | tf_op jit(solution)/shard_map/reduce_scatter | solution.py:139
  380.6 2.3 select_convert_fusion
  383.0 0.0 all-gather.9.cloned.1.call-update
  383.0 29.4 %all-gather.9.cloned.1.call-done = bf16[1024,1600]{0,1:T(8,128)(2,1)} async-done(((bf16[1024,400]{0,1:T(8,128)(2,1)}), bf16[1024,1600]{0,1:T(8,128)(2,1)}) %all-gather.9.cloned.1.call-update) | async-done | bytes 3276816 | tf_op jit(solution)/shard_map/all_gather | solution.py:144
  412.4 2.7 convert_reduce_fusion
  415.1 2.8 fusion.4
  418.0 1.6 fusion.75
  419.6 0.9 copy.48
  420.5 1.4 convolution_convert_fusion.1
  422.0 2.2 copy.36
  424.2 5.5 all-to-all-start.3
  429.7 0.0 all-gather.11.cloned.1.call-start
  429.7 0.5 all-gather.11.cloned.1.call-update
  430.3 123.2 %all-to-all-done.3 = bf16[8,128,1600]{1,2,0:T(8,128)(2,1)} async-done(((bf16[8,128,1600]{1,2,0:T(8,128)(2,1)}), bf16[8,128,1600]{1,2,0:T(8,128)(2,1)}, u32[]{:S(2)}, u32[]{:S(2)}) %all-to-all-start.3) | async-done | bytes 3276832 | tf_op jit(solution)/shard_map/all_to_all | solution.py:38
  553.5 2.6 fusion.42
  556.1 1.8 bitcast_convert_fusion.1
  557.9 59.8 %all_to_all.34 = bf16[8,128,1200]{1,2,0:T(8,128)(2,1)S(1)} all-to-all(bf16[8,128,1200]{1,2,0:T(8,128)(2,1)S(1)} %bitcast_convert_fusion.1), channel_id=1, replica_groups=mesh['row'=8,'col'=4] {'row'}, dimensions={0} | all-to-all | bytes 4915200 | tf_op jit(solution)/shard_map/all_to_all | solution.py:56
  617.8 0.8 fusion.33
  618.6 2.4 convert_element_type.116
  621.0 10.9 %fusion.21 = bf16[1024,1200]{0,1:T(8,128)(2,1)} fusion(f32[150,8,8,128]{3,2,1,0:T(8,128)} %bitcast.94, bf16[1600,1200]{1,0:T(8,128)(2,1)} %all-gather.11.cloned.1.call-done, f32[1200]{0:T(1024)S(1)} %copy-done.13, pred[1024]{0:T(1024)(128)(4,1)S(1)} %fusion.64, bf16[1024,1600]{0,1:T(8,128)(2,1)S(1)} %copy-done.2, f32[1600]{0:T(1024)S(1)} %copy-done.9, ...), kind=kOutput, calls=%fused_computation.29 | convolution fusion | flops 3946905600 | bytes 14516416 | tf_op jit(solution)/shard_map/dot_general | solution.py:16
  (40 shorter events, 0.1 us)
Async XLA Ops:
  7.2 173.1 %copy-start = (bf16[4,16,1600]{2,1,0:T(8,128)(2,1)S(1)}, bf16[4,16,1600]{2,1,0:T(8,128)(2,1)}, u32[]{:S(2)}) copy-start(bf16[4,16,1600]{2,1,0:T(8,128)(2,1)} %param.30) | copy-start | bytes 614404
  7.2 37.9 %copy-start.4 = (bf16[1024,400]{0,1:T(8,128)(2,1)S(1)}, bf16[1024,400]{0,1:T(8,128)(2,1)}, u32[]{:S(2)}) copy-start(bf16[1024,400]{0,1:T(8,128)(2,1)} %param.18) | copy-start | bytes 2457604
  7.2 309.0 %all-gather.5.cloned.1.call-start = ((), (), s32[]{:S(2)}) async-start(), calls=%async_computation.6 | async-start | bytes 5990400 | tf_op jit(solution)/shard_map/all_gather | solution.py:120
  7.2 12.7 %collective-permute-start = (bf16[1024,400]{0,1:T(8,128)(2,1)}, bf16[1024,400]{0,1:T(8,128)(2,1)S(1)}, u32[]{:S(2)}, u32[]{:S(2)}) collective-permute-start(bf16[1024,400]{0,1:T(8,128)(2,1)} %param.18), channel_id=1, source_target_pairs={{0,1},{1,2},{2,3},{3,0},{4,5},{5,6},{6,7},{7,4},{8,9},{9,10},{10,1... | collective-permute-start | bytes 2457608 | tf_op jit(solution)/shard_map/ppermute | solution.py:94
  19.9 11.8 %collective-permute-start.1 = (bf16[1024,400]{0,1:T(8,128)(2,1)S(1)}, bf16[1024,400]{0,1:T(8,128)(2,1)S(1)}, u32[]{:S(2)}, u32[]{:S(2)}) collective-permute-start(bf16[1024,400]{0,1:T(8,128)(2,1)S(1)} %collective-permute-done), channel_id=1, source_target_pairs={{0,1},{1,2},{2,3},{3,0},{4,5},{5,6},{6,7},{7,4},{8,9},{9,10},{10,1... | collective-permute-start | bytes 2457608 | tf_op jit(solution)/shard_map/ppermute | solution.py:94
  31.7 11.8 %collective-permute-start.2 = (bf16[1024,400]{0,1:T(8,128)(2,1)S(1)}, bf16[1024,400]{0,1:T(8,128)(2,1)S(1)}, u32[]{:S(2)}, u32[]{:S(2)}) collective-permute-start(bf16[1024,400]{0,1:T(8,128)(2,1)S(1)} %collective-permute-done.1), channel_id=1, source_target_pairs={{0,1},{1,2},{2,3},{3,0},{4,5},{5,6},{6,7},{7,4},{8,9},{9,10},{10,1... | collective-permute-start | bytes 2457608 | tf_op jit(solution)/shard_map/ppermute | solution.py:94
  33.5 21.0 %all-to-all-start.1 = ((bf16[8,1,4]{2,1,0:T(2,128)(2,1)}), bf16[8,1,4]{2,1,0:T(2,128)(2,1)S(1)}, u32[]{:S(2)}, u32[]{:S(2)}) async-start(bf16[8,1,4]{2,1,0:T(2,128)(2,1)} %copy.30), calls=%async_computation.1 | async-start | bytes 8192 | tf_op jit(solution)/shard_map/all_to_all | solution.py:39
  44.9 3.0 copy-start.7
  44.9 3.0 copy-start.8
  45.1 2.7 copy-start.3
  54.5 124.1 %all-to-all-start = ((bf16[8,128,1600]{1,2,0:T(8,128)(2,1)}), bf16[8,128,1600]{1,2,0:T(8,128)(2,1)S(1)}, u32[]{:S(2)}, u32[]{:S(2)}) async-start(bf16[8,128,1600]{1,2,0:T(8,128)(2,1)} %copy.29), calls=%async_computation | async-start | bytes 6553600 | tf_op jit(solution)/shard_map/all_to_all | solution.py:38
  61.1 271.6 %all-gather.7.cloned.1.call-start = ((), (), s32[]{:S(2)}) async-start(), calls=%async_computation.7 | async-start | bytes 5990400 | tf_op jit(solution)/shard_map/all_gather | solution.py:136
  61.8 318.8 %reduce-scatter.2.cloned.1.call-start = ((), (), s32[]{:S(2)}) async-start(), calls=%async_computation.8 | async-start | bytes 4096000 | tf_op jit(solution)/shard_map/reduce_scatter | solution.py:139
  313.2 3.0 copy-start.12
  332.6 10.9 %copy-start.14 = (s32[8]{0:T(128)S(1)}, s32[8]{0:T(128)}, u32[]{:S(2)}) copy-start(s32[8]{0:T(128)} %param.35) | copy-start | bytes 100
  332.6 48.0 %copy-start.5 = (bf16[1024,400]{0,1:T(8,128)(2,1)S(1)}, bf16[1024,400]{0,1:T(8,128)(2,1)}, u32[]{:S(2)}) copy-start(bf16[1024,400]{0,1:T(8,128)(2,1)} %param.18) | copy-start | bytes 2457604
  332.6 48.0 %copy-start.11 = (f32[400]{0:T(512)S(1)}, f32[400]{0:T(512)}, u32[]{:S(2)}) copy-start(f32[400]{0:T(512)} %param.22) | copy-start | bytes 4804
  343.4 74.5 %copy-start.9 = (f32[1600]{0:T(1024)S(1)}, f32[1600]{0:T(1024)}, u32[]{:S(2)}) copy-start(f32[1600]{0:T(1024)} %param.28) | copy-start | bytes 19204
  343.4 74.6 %copy-start.10 = (f32[1600]{0:T(1024)S(1)}, f32[1600]{0:T(1024)}, u32[]{:S(2)}) copy-start(f32[1600]{0:T(1024)} %param.27) | copy-start | bytes 19204
  343.4 69.0 %all-gather.9.cloned.1.call-start = ((), (), s32[]{:S(2)}) async-start(), calls=%async_computation.9 | async-start | bytes 4096000 | tf_op jit(solution)/shard_map/all_gather | solution.py:144
  412.4 5.6 copy-start.2
  421.9 131.5 %copy-start.6 = (bf16[4,16,1600]{2,1,0:T(8,128)(2,1)S(1)}, bf16[4,16,1600]{2,1,0:T(8,128)(2,1)}, u32[]{:S(2)}) copy-start(bf16[4,16,1600]{2,1,0:T(8,128)(2,1)} %param.31) | copy-start | bytes 614404
  424.2 129.3 %all-to-all-start.3 = ((bf16[8,128,1600]{1,2,0:T(8,128)(2,1)}), bf16[8,128,1600]{1,2,0:T(8,128)(2,1)}, u32[]{:S(2)}, u32[]{:S(2)}) async-start(bf16[8,128,1600]{1,2,0:T(8,128)(2,1)} %copy.36), calls=%async_computation.4 | async-start | bytes 6553600 | tf_op jit(solution)/shard_map/all_to_all | solution.py:38
  429.7 191.4 %all-gather.11.cloned.1.call-start = ((), (), s32[]{:S(2)}) async-start(), calls=%async_computation.10 | async-start | bytes 4608000 | tf_op jit(solution)/shard_map/all_gather | solution.py:149
  617.8 3.3 copy-start.13
  621.0 10.9 %copy-start.1 = (bf16[4,16,1600]{2,1,0:T(8,128)(2,1)S(1)}, bf16[4,16,1600]{2,1,0:T(8,128)(2,1)}, u32[]{:S(2)}) copy-start(bf16[4,16,1600]{2,1,0:T(8,128)(2,1)} %param.30) | copy-start | bytes 614404
Sparse Core Ops, SparseCore 0:
  20.1 143.1 all-gather.4
  165.5 141.3 all-gather.6
  343.6 36.9 reduce-scatter.1
  383.1 29.2 all-gather.8
  432.6 123.5 all-gather.10
